TPU v7x, 128 devices: a whole 4x4x4 slice. The times are simulated.
128 devices in a mesh: ij: 2 (over x_lo), ab: 16 (over y, x_hi, core), cd: 4 (over z).
Axes of the slice: x: 4 (x_hi: 2, x_lo: 2; x = x_hi * 2 + x_lo), y: 4, z: 4, core: 2. Of those that a mesh axis runs over, the one named last changes fastest.
Arguments:
- amplitudes: float32 [2048, 16384], P('ab', ('ij', 'cd')), may hold values from -6 to 6
- integrals: float32 [16384, 16384], P('ab', ('ij', 'cd')), may hold values from -0.046875 to 0.046875
- occupied_label: int32 [16], replicated, may hold values from 0 to 3
- outer_label: int32 [128], replicated, may hold values from 0 to 3
- inner_label: int32 [128], replicated, may hold values from 0 to 3
Outputs:
- ladder_term: float32 [2048, 16384], P(('ij', 'cd'), 'ab')
Inputs may be any that keep to these rules, and one draw needn't show every extreme that they name: `occupied_label`: each label names the symmetry block of one tile; tiles couple only where labels agree. `outer_label`: labels of the outer tiles, as above. `inner_label`: labels of the contracted tiles, as above.
All inputs are finite; a program needn't handle non-finite values.
Results may differ from a plain program's by a relative error of at most 0.000073.
Values sent between devices are 32-bit elements; how exact they have to be, the bound alone decides.
No kernel may reach another device: no remote copies, remote signals or barrier semaphores. Data moves between devices by JAX's collectives and lax.ppermute only.
A program may use at most 192 MiB of HBM per device.

v0:
```python
import jax
import jax.numpy as jnp
from jax import lax
from jax.sharding import PartitionSpec as P

TILE = 128


def contract(left, right):
    return lax.dot_general(
        left,
        right,
        (((1,), (1,)), ((), ())),
        precision=lax.Precision.HIGHEST,
        preferred_element_type=jnp.float32,
    )


def shards(amplitudes, integrals, occupied_label, outer_label, inner_label):
    size_cd = lax.axis_size("cd")
    pos_ij = lax.axis_index("ij")
    pos_ab = lax.axis_index("ab")
    pos_cd = lax.axis_index("cd")
    amp_rows_here = amplitudes.shape[0]
    col_count = amplitudes.shape[1]
    int_rows_here = integrals.shape[0]
    col_start = (pos_ij * size_cd + pos_cd) * col_count
    inner_here = lax.dynamic_slice_in_dim(jnp.repeat(inner_label, TILE), col_start, col_count)
    occupied_here = lax.dynamic_slice_in_dim(
        jnp.repeat(occupied_label, TILE), pos_ab * amp_rows_here, amp_rows_here
    )
    outer_here = lax.dynamic_slice_in_dim(
        jnp.repeat(outer_label, TILE), pos_ab * int_rows_here, int_rows_here
    )
    amp_masked = jnp.where(
        occupied_here[:, None] == inner_here[None, :], amplitudes, jnp.zeros((), amplitudes.dtype)
    )
    int_masked = jnp.where(
        outer_here[:, None] == inner_here[None, :], integrals, jnp.zeros((), integrals.dtype)
    )
    all_rows = lax.all_gather(amp_masked, "ab", axis=0, tiled=True)
    own_pairs = lax.all_to_all(all_rows, "ij", split_axis=0, concat_axis=1, tiled=True)
    partial_sum = contract(own_pairs, lax.all_gather(int_masked, "ij", axis=1, tiled=True))
    return lax.psum_scatter(partial_sum, "cd", scatter_dimension=0, tiled=True)


def solution(mesh):
    placed = (P("ab", ("ij", "cd")), P("ab", ("ij", "cd")), P(), P(), P())
    return jax.shard_map(
        shards, mesh=mesh, in_specs=placed, out_specs=P(("ij", "cd"), "ab"), check_vma=False
    )
```

profile of v0, /device:TPU:20, one launch (start us, length us, event | category | flops | bytes accessed | tf_op | source)
XLA Modules:
  0.0 687.3 jit_solution(11336803445629982448)
XLA Ops:
  6.5 0.0 copy-start
  6.5 0.0 all-gather.3.cloned.1.call-start
  6.5 0.7 broadcast_bitcast_fusion.2
  7.3 0.0 copy-done
  7.3 0.1 broadcast_bitcast_fusion.1
  7.4 0.1 dynamic_slice.9
  7.4 2.3 compare_select_fusion.1
  9.8 0.0 all-gather.3.cloned.1.call-update
  9.8 0.0 all-gather.5.cloned.1.call-start
  9.9 0.7 broadcast_bitcast_fusion
  10.6 7.3 %compare_select_fusion = f32[1024,2048]{1,0:T(8,128)} fusion(f32[1024,2048]{1,0:T(8,128)} %param.6, s32[2048]{0:T(1024)S(1)} %dynamic_slice.10, s32[1024]{0:T(1024)S(1)} %dynamic_slice.11), kind=kLoop, calls=%fused_computation | loop fusion | flops 4194304 | bytes 16789504 | tf_op jit(solution)/shard_map/jit(_where)/select_n | solution.py:38
  17.9 0.0 all-gather.5.cloned.1.call-update
  17.9 0.0 reduce-scatter.2.cloned.1.call-start
  18.0 99.1 %all-gather.3.cloned.1.call-done = f32[2048,2048]{1,0:T(8,128)} async-done(((f32[128,2048]{1,0:T(8,128)}), f32[2048,2048]{1,0:T(8,128)}) %all-gather.3.cloned.1.call-update) | async-done | bytes 16777232 | tf_op jit(solution)/shard_map/all_gather | solution.py:41
  117.1 379.1 %all_to_all.19 = f32[2,1024,2048]{2,1,0:T(8,128)} all-to-all(f32[2,1024,2048]{2,1,0:T(8,128)} %bitcast.12), channel_id=1, replica_groups=mesh['ij'=2,'ab'=16,'cd'=4] {'ij'}, dimensions={0} | all-to-all | bytes 33554432 | tf_op jit(solution)/shard_map/all_to_all | solution.py:42
  496.2 18.0 %copy.6 = f32[1024,2,2048]{0,2,1:T(8,128)} copy(f32[1024,2,2048]{2,0,1:T(8,128)} %bitcast.11) | data formatting | bytes 33554432 | tf_op jit(solution)/shard_map/all_to_all | solution.py:42
  514.2 0.0 all-gather.5.cloned.1.call-done
  514.2 0.0 copy-start.1
  514.2 115.8 %fusion = f32[1024,1024]{1,0:T(8,128)} fusion(f32[1024,4096]{0,1:T(8,128)} %bitcast.13, f32[1024,4096]{1,0:T(8,128)} %all-gather.5.cloned.1.call-done), kind=kOutput, calls=%fused_computation.5 | convolution fusion | flops 51539607552 | bytes 37748736 | tf_op jit(solution)/shard_map/dot_general | solution.py:10
  630.0 0.0 reduce-scatter.2.cloned.1.call-update
  630.0 50.7 %reduce-scatter.2.cloned.1.call-done = f32[256,1024]{1,0:T(8,128)} async-done(((f32[1024,1024]{1,0:T(8,128)}), f32[256,1024]{1,0:T(8,128)}) %reduce-scatter.2.cloned.1.call-update) | async-done | bytes 1048592 | tf_op jit(solution)/shard_map/reduce_scatter | solution.py:44
  680.8 0.0 copy-done.1
  (2 shorter events, 0.0 us)
Async XLA Ops:
  6.5 0.7 copy-start
  6.5 110.6 %all-gather.3.cloned.1.call-start = ((), (), s32[]{:S(2)}) async-start(), calls=%async_computation.2 | async-start | bytes 17825792 | tf_op jit(solution)/shard_map/all_gather | solution.py:41
  9.8 504.4 %all-gather.5.cloned.1.call-start = ((), (), s32[]{:S(2)}) async-start(), calls=%async_computation.3 | async-start | bytes 25165824 | tf_op jit(solution)/shard_map/all_gather | solution.py:43
  17.9 662.8 %reduce-scatter.2.cloned.1.call-start = ((), (), s32[]{:S(2)}) async-start(), calls=%async_computation.4 | async-start | bytes 5242880 | tf_op jit(solution)/shard_map/reduce_scatter | solution.py:44
  514.2 166.6 %copy-start.1 = (s32[128]{0:T(128)S(1)}, s32[128]{0:T(128)}, u32[]{:S(2)}) copy-start(s32[128]{0:T(128)} %param.9) | copy-start | bytes 1540
Sparse Core Ops, SparseCore 0:
  9.9 107.1 all-gather.2
  118.8 380.0 all-gather.4
  630.1 50.5 reduce-scatter.1
where the time goes:
time: 689 us; the launch traced here: 687 us
  blocking collectives  379 us (55%)
  waiting for transfers between devices  150 us (22%)
  matrix products  116 us (17%)
  local copies, waits for them, and re-layouts  19.6 us (3%)
  between operations  13.1 us (2%)
  other arithmetic  9.64 us (1%)
    all_to_all x1, blocking collectives, shards(): lax.all_to_all(all_rows, 'ij', split_axis=0, concat_axis=1, tiled=True)  379 us
    dot_general x1, matrix products, contract(): lax.dot_general(left, right, (((1,), (1,)), ((), ())), precision=lax.Prec...  116 us
    all_gather x1, waiting for transfers between devices, shards(): all_rows = lax.all_gather(amp_masked, 'ab', axis=0, tiled=True)  99.1 us
    reduce_scatter x1, waiting for transfers between devices, shards(): return lax.psum_scatter(partial_sum, 'cd', scatter_dimension=0, tiled=True)  50.7 us
    all_to_all x1, local copies, waits for them, and re-layouts, shards(): lax.all_to_all(all_rows, 'ij', split_axis=0, concat_axis=1, tiled=True)  18 us
  transfers between devices with their start and end apart: 3, of which 2 were waited for; matrix products, arithmetic and copies ran while one was open for 4% of the time, Pallas kernels for 0%

commit v1 on v0

v1 whole, which is shorter than its diff:
```python
import functools

import jax
import jax.numpy as jnp
from jax import lax
from jax.experimental import pallas as pl
from jax.experimental.pallas import tpu as pltpu
from jax.sharding import PartitionSpec as P

TILE = 128
LABELS = 4
CAPS_T = (8, 12, 16)
CAPS_R = ((12, 8), (16, 13), (22, 14), (32, 16))
ROWS = 16
COLS = 16
OUTS = 8
SMEM = pl.BlockSpec(memory_space=pltpu.SMEM)
HBM = pl.BlockSpec(memory_space=pl.ANY)
VMEM = pl.BlockSpec(memory_space=pltpu.VMEM)


def ab_index(y, xh, k):
    return y * 4 + xh * 2 + k


PLACES = [(y, xh, k) for y in range(4) for xh in range(2) for k in range(2)]
CORE_SWAP = [(ab_index(y, x, k), ab_index(y, x, 1 - k)) for y, x, k in PLACES]
X_SWAP = [(ab_index(y, x, k), ab_index(y, 1 - x, k)) for y, x, k in PLACES]
Y_UP = [(ab_index(y, x, k), ab_index((y + 1) % 4, x, k)) for y, x, k in PLACES]
Y_DOWN = [(ab_index(y, x, k), ab_index((y + 3) % 4, x, k)) for y, x, k in PLACES]
Z_UP = [(c, (c + 1) % 4) for c in range(4)]
Z_DOWN = [(c, (c + 3) % 4) for c in range(4)]


def where_am_i():
    block = lax.axis_index("ij") * 4 + lax.axis_index("cd")
    device_row = lax.axis_index("ab")
    return block, device_row, device_row // 4, (device_row // 2) % 2, device_row % 2


def count_labels(labels, first, size, counts, base):
    for label in range(LABELS):
        counts[base + label] = 0

    def add(at, carry):
        counts[base + labels[first + at]] += 1
        return carry

    lax.fori_loop(0, size, add, 0)


def plan_kernel(occ, outer, inner, amp_pick, out_pick, first_rows, counts):
    def amp_block(block, need):
        count_labels(inner, block * COLS, COLS, counts, 0)

        def chip_need(chip, need):
            return jnp.maximum(need, counts[occ[2 * chip]] + counts[occ[2 * chip + 1]])

        return lax.fori_loop(0, ROWS // 2, chip_need, need)

    need = lax.fori_loop(0, 8, amp_block, jnp.int32(0))
    pick = jnp.int32(0)
    for cap in CAPS_T[:-1]:
        pick += (need > 2 * cap).astype(jnp.int32)
    amp_pick[0] = pick

    def out_block(block, needs):
        count_labels(outer, block * OUTS, OUTS, counts, 0)

        def dest(c, needs):
            need_w, need_z = needs
            low = counts[occ[2 * c]] + counts[occ[2 * c + 1]]
            high = counts[occ[2 * c + 8]] + counts[occ[2 * c + 9]]
            return jnp.maximum(need_w, jnp.maximum(low, high)), jnp.maximum(need_z, low + high)

        return lax.fori_loop(0, 4, dest, needs)

    need_w, need_z = lax.fori_loop(0, ROWS, out_block, (jnp.int32(0), jnp.int32(0)))
    pick = jnp.int32(0)
    for cap_z, cap_w in CAPS_R[:-1]:
        pick += jnp.logical_or(need_w > cap_w, need_z > cap_z).astype(jnp.int32)
    out_pick[0] = pick
    count_labels(outer, lax.axis_index("ab") * OUTS, OUTS, counts, 0)
    c = lax.axis_index("cd")
    first_rows[0] = counts[occ[2 * c]] + counts[occ[2 * c + 1]]


def plan(occ, outer, inner):
    one = jax.ShapeDtypeStruct((1,), jnp.int32)
    return pl.pallas_call(
        plan_kernel,
        out_shape=(one, one, one),
        in_specs=[SMEM] * 3,
        out_specs=(SMEM, SMEM, SMEM),
        scratch_shapes=[pltpu.SMEM((LABELS,), jnp.int32)],
        name="plan_capacities",
    )(occ, outer, inner)


def pack_kernel(occ, inner, mine, other, packed, sem):
    block, _, y, xh, k = where_am_i()
    chip = y * 2 + xh

    def tile(ref, c):
        return ref.at[:, pl.ds(pl.multiple_of(c * TILE, TILE), TILE)]

    def issue(core, first):
        label = occ[chip * 2 + core]

        def one(c, p):
            hit = inner[block * COLS + c] == label

            @pl.when(jnp.logical_and(hit, core == k))
            def _():
                pltpu.make_async_copy(tile(mine, c), packed.at[p], sem.at[p]).start()

            @pl.when(jnp.logical_and(hit, core != k))
            def _():
                pltpu.make_async_copy(tile(other, c), packed.at[p], sem.at[p]).start()

            return p + hit.astype(jnp.int32)

        return lax.fori_loop(0, COLS, one, first)

    count = issue(1, issue(0, jnp.int32(0)))

    def drain(p, carry):
        pltpu.make_async_copy(tile(mine, 0), packed.at[p], sem.at[p]).wait()
        return carry

    lax.fori_loop(0, count, drain, 0)


def pack(occ, inner, mine, other):
    return pl.pallas_call(
        pack_kernel,
        out_shape=jax.ShapeDtypeStruct((2 * COLS, TILE, TILE), jnp.float32),
        in_specs=[SMEM, SMEM, HBM, HBM],
        out_specs=HBM,
        scratch_shapes=[pltpu.SemaphoreType.DMA((2 * COLS,))],
        name="pack_amplitudes",
    )(occ, inner, mine, other)


def split(x):
    hi = x.astype(jnp.bfloat16)
    lo = (x - hi.astype(jnp.float32)).astype(jnp.bfloat16)
    return hi, lo


def split_kernel(outer, inner, ints, hi, lo, buf, sem):
    block, device_row, _, _, _ = where_am_i()
    col0 = block * COLS
    out0 = device_row * OUTS

    def copy(t, c, p):
        return pltpu.make_async_copy(
            ints.at[pl.ds(pl.multiple_of(t * TILE, TILE), TILE), pl.ds(pl.multiple_of(c * TILE, TILE), TILE)],
            buf.at[t * COLS + p],
            sem.at[t * COLS + p],
        )

    def count(t, use):
        label = outer[out0 + t]

        def one(c, p):
            hit = inner[col0 + c] == label
            if use:

                @pl.when(hit)
                def _():
                    copy(t, c, p).start()

            return p + hit.astype(jnp.int32)

        return lax.fori_loop(0, COLS, one, jnp.int32(0))

    def issue(t, carry):
        count(t, True)
        return carry

    lax.fori_loop(0, OUTS, issue, 0)

    def split_all(t, carry):
        def one(p, inner_carry):
            copy(t, 0, p).wait()
            at = t * COLS + p
            hi[at], lo[at] = split(buf[at])
            return inner_carry

        return lax.fori_loop(0, count(t, False), one, carry)

    lax.fori_loop(0, OUTS, split_all, 0)


def split_integrals(outer, inner, ints):
    part = jax.ShapeDtypeStruct((OUTS * COLS, TILE, TILE), jnp.bfloat16)
    return pl.pallas_call(
        split_kernel,
        out_shape=(part, part),
        in_specs=[SMEM, SMEM, HBM],
        out_specs=(VMEM, VMEM),
        scratch_shapes=[
            pltpu.VMEM((OUTS * COLS, TILE, TILE), jnp.float32),
            pltpu.SemaphoreType.DMA((OUTS * COLS,)),
        ],
        compiler_params=pltpu.CompilerParams(vmem_limit_bytes=20 * 1024 * 1024),
        cost_estimate=pl.CostEstimate(flops=1 << 24, bytes_accessed=16 << 20, transcendentals=0),
        name="split_integrals",
    )(outer, inner, ints)


def pieces(cap):
    half = cap // 2
    rest = cap - half
    same = [
        (1, 0, cap, 0, 0, 1, 0),
        (2, 0, cap, 0, 3, 0, 0),
        (3, 0, cap, 0, 1, 0, 0),
        (4, 0, cap, 0, 3, 1, 0),
        (4, cap, half, 0, 2, 0, 0),
        (5, 0, cap, 0, 1, 1, 0),
        (5, cap, rest, 0, 2, 0, half),
        (6, 0, half, 0, 2, 1, 0),
        (7, 0, rest, 0, 2, 1, half),
    ]
    start = {1: (8, 0), 2: (8, cap), 3: (8, 2 * cap), 4: (9, 0), 5: (9, cap + half), 6: (10, 0), 7: (10, half)}
    swapped = [
        (start[at][0], start[at][1] + offset, size, 1, dy, dx, first)
        for at, offset, size, _, dy, dx, first in same
    ]
    return same + swapped


def ladder_kernel(cap, occ, outer, inner, ints_hi, ints_lo, *refs):
    lists = refs[:11]
    part, amp_buf, int_hi, int_lo, out_buf, row_n, row_at, out_n, out_at, in_n, amp_sem, int_sem, out_sem = refs[11:]
    block, device_row, y, xh, k = where_am_i()
    col0 = block * COLS
    out0 = device_row * OUTS

    int_copies = [
        pltpu.make_async_copy(ints_hi, int_hi, int_sem.at[0]),
        pltpu.make_async_copy(ints_lo, int_lo, int_sem.at[1]),
    ]
    for copy in int_copies:
        copy.start()
    count_labels(inner, col0, COLS, in_n, 0)

    def fill_amps(src, offset, size, chip, first):
        used = in_n[occ[2 * chip]] + in_n[occ[2 * chip + 1]]

        def one(q, carry):
            at = chip * 2 * cap + first + q
            pltpu.make_async_copy(src.at[offset + q], amp_buf.at[at], amp_sem.at[at]).start()
            return carry

        lax.fori_loop(0, jnp.clip(used - first, 0, size), one, 0)

    fill_amps(lists[0], 0, 2 * cap, y * 2 + xh, 0)
    for at, offset, size, swapped, dy, dx, first in pieces(cap):
        core = k ^ swapped
        fill_amps(lists[at], offset, size, ((y + dy) % 4) * 2 + (xh + dx) % 2, core * cap + first)

    for label in range(LABELS):
        row_n[label] = 0
        out_n[label] = 0

    def list_rows(r, carry):
        label = occ[r]
        row_at[label * ROWS + row_n[label]] = r
        row_n[label] += 1
        return carry

    lax.fori_loop(0, ROWS, list_rows, 0)

    def list_outs(t, carry):
        label = outer[out0 + t]
        out_at[label * OUTS + out_n[label]] = t
        out_n[label] += 1
        return carry

    lax.fori_loop(0, OUTS, list_outs, 0)

    def wait_amps(chip, carry):
        def one(p, inner_carry):
            at = chip * 2 * cap + p
            pltpu.make_async_copy(lists[0].at[0], amp_buf.at[at], amp_sem.at[at]).wait()
            return inner_carry

        return lax.fori_loop(0, in_n[occ[2 * chip]] + in_n[occ[2 * chip + 1]], one, carry)

    lax.fori_loop(0, ROWS // 2, wait_amps, 0)
    for copy in int_copies:
        copy.wait()

    def out_copy(dest, slot):
        return pltpu.make_async_copy(
            out_buf.at[dest * 4 * OUTS + slot], part.at[dest, slot], out_sem.at[dest * 4 * OUTS + slot]
        )

    def per_label(label, carry):
        n_rows, n_outs, n_in = row_n[label], out_n[label], in_n[label]

        def block_of(buf, at0, at1, p, width):
            return jnp.concatenate(
                [jnp.concatenate([buf[at + p + w] for w in range(width)], axis=1) for at in (at0, at1)], axis=0
            )

        def per_rows(rp, carry):
            m0 = 2 * rp
            m1 = jnp.minimum(m0 + 1, n_rows - 1)
            r0, r1 = row_at[label * ROWS + m0], row_at[label * ROWS + m1]

            def list_start(r):
                chip = r // 2
                return chip * 2 * cap + jnp.where(r % 2 == 1, in_n[occ[2 * chip]], 0)

            a0, a1 = list_start(r0), list_start(r1)

            def per_outs(up, carry):
                q0 = 2 * up
                q1 = jnp.minimum(q0 + 1, n_outs - 1)
                b0, b1 = out_at[label * OUTS + q0] * COLS, out_at[label * OUTS + q1] * COLS

                def step(width, first):
                    def run(pp, total):
                        p = first + pp * width
                        left_hi, left_lo = split(block_of(amp_buf, a0, a1, p, width))
                        right_hi, right_lo = block_of(int_hi, b0, b1, p, width), block_of(int_lo, b0, b1, p, width)

                        def dot(a, b):
                            return lax.dot_general(
                                a, b, (((1,), (1,)), ((), ())), preferred_element_type=jnp.float32
                            )

                        return total + (dot(left_lo, right_hi) + dot(left_hi, right_lo) + dot(left_hi, right_hi))

                    return run

                total = jnp.zeros((2 * TILE, 2 * TILE), jnp.float32)
                total = lax.fori_loop(0, n_in // 2, step(2, 0), total)
                total = lax.fori_loop(0, n_in % 2, step(1, n_in // 2 * 2), total)
                for rr in range(2):
                    r = (r0, r1)[rr]
                    dest = (r // 2) % 4
                    before = jnp.where(r % 2 == 1, out_n[occ[r // 2 * 2]], 0)
                    low = out_n[occ[dest * 2]] + out_n[occ[dest * 2 + 1]]
                    before += jnp.where(r >= 8, low, 0)
                    for tt in range(2):
                        fresh = jnp.bool_(True)
                        if rr:
                            fresh = jnp.logical_and(fresh, m1 > m0)
                        if tt:
                            fresh = jnp.logical_and(fresh, q1 > q0)
                        value = total[rr * TILE : (rr + 1) * TILE, tt * TILE : (tt + 1) * TILE]

                        @pl.when(fresh)
                        def _(dest=dest, slot=before + (q0, q1)[tt], value=value):
                            out_buf[dest * 4 * OUTS + slot] = value
                            out_copy(dest, slot).start()

                return carry

            return lax.fori_loop(0, (n_outs + 1) // 2, per_outs, carry)

        return lax.fori_loop(0, (n_rows + 1) // 2, per_rows, carry)

    lax.fori_loop(0, LABELS, per_label, 0)

    def drain_outs(dest, carry):
        def drain(slot, inner_carry):
            out_copy(dest, slot).wait()
            return inner_carry

        count = jnp.int32(0)
        for r in (0, 1, 8, 9):
            count += out_n[occ[dest * 2 + r]]
        return lax.fori_loop(0, count, drain, carry)

    lax.fori_loop(0, 4, drain_outs, 0)


def ladder(cap, occ, outer, inner, ints_hi, ints_lo, lists):
    amps = ROWS * cap
    return pl.pallas_call(
        functools.partial(ladder_kernel, cap),
        out_shape=jax.ShapeDtypeStruct((4, 4 * OUTS, TILE, TILE), jnp.float32),
        in_specs=[SMEM] * 3 + [HBM] * (2 + len(lists)),
        out_specs=HBM,
        scratch_shapes=[
            pltpu.VMEM((amps, TILE, TILE), jnp.float32),
            pltpu.VMEM((OUTS * COLS, TILE, TILE), jnp.bfloat16),
            pltpu.VMEM((OUTS * COLS, TILE, TILE), jnp.bfloat16),
            pltpu.VMEM((OUTS * COLS, TILE, TILE), jnp.float32),
            pltpu.SMEM((LABELS,), jnp.int32),
            pltpu.SMEM((LABELS * ROWS,), jnp.int32),
            pltpu.SMEM((LABELS,), jnp.int32),
            pltpu.SMEM((LABELS * OUTS,), jnp.int32),
            pltpu.SMEM((LABELS,), jnp.int32),
            pltpu.SemaphoreType.DMA((amps,)),
            pltpu.SemaphoreType.DMA((2,)),
            pltpu.SemaphoreType.DMA((OUTS * COLS,)),
        ],
        compiler_params=pltpu.CompilerParams(vmem_limit_bytes=(18 + cap) * 1024 * 1024),
        name="ladder_tiles",
    )(occ, outer, inner, ints_hi, ints_lo, *lists)


def gather_and_multiply(cap, packed, occ, outer, inner, ints):
    half = cap // 2
    core = lax.axis_index("ab") % 2
    send = functools.partial(lax.ppermute, axis_name="ab")
    own = lax.dynamic_slice_in_dim(packed, core * cap, cap)
    x_own = send(own, perm=X_SWAP)
    up = send(own, perm=Y_UP)
    down = send(own, perm=Y_DOWN)
    up_two = send(jnp.concatenate([x_own, up[:half]]), perm=Y_UP)
    down_two = send(jnp.concatenate([x_own, down[half:]]), perm=Y_DOWN)
    ints_hi, ints_lo = split_integrals(outer, inner, ints)
    up_two, down_two, ints_hi, ints_lo = lax.optimization_barrier((up_two, down_two, ints_hi, ints_lo))
    up_three = send(up_two[:half], perm=Y_UP)
    down_three = send(down_two[half:cap], perm=Y_DOWN)
    lists = [packed, x_own, up, down, up_two, down_two, up_three, down_three]
    lists.append(send(jnp.concatenate([x_own, up, down]), perm=CORE_SWAP))
    lists.append(send(jnp.concatenate([up_two, down_two]), perm=CORE_SWAP))
    lists.append(send(jnp.concatenate([up_three, down_three]), perm=CORE_SWAP))
    return ladder(cap, occ, outer, inner, ints_hi, ints_lo, lists)


def place_kernel(cap_z, cap_w, occ, outer, first_rows, mine, other, out):
    block, device_row, _, _, _ = where_am_i()
    skip = jnp.maximum(first_rows[0] - (cap_z - cap_w), 0)
    slot = jnp.where(block >= 4, skip, 0)
    for r in range(2):
        label = occ[block * 2 + r]
        for t in range(OUTS):
            hit = outer[device_row * OUTS + t] == label
            at = jnp.minimum(slot, cap_w - 1)
            value = mine[at] + other[at]
            out[r * TILE : (r + 1) * TILE, t * TILE : (t + 1) * TILE] = jnp.where(
                hit, value, jnp.zeros_like(value)
            )
            slot = slot + hit.astype(jnp.int32)


def place(cap_z, cap_w, occ, outer, first_rows, mine, other):
    return pl.pallas_call(
        functools.partial(place_kernel, cap_z, cap_w),
        out_shape=jax.ShapeDtypeStruct((2 * TILE, OUTS * TILE), jnp.float32),
        in_specs=[SMEM] * 3 + [VMEM] * 2,
        out_specs=VMEM,
        compiler_params=pltpu.CompilerParams(vmem_limit_bytes=16 * 1024 * 1024),
        name="place_tiles",
    )(occ, outer, first_rows, mine, other)


def reduce_and_place(caps, part, occ, outer, first_rows):
    cap_z, cap_w = caps
    half = cap_z // 2
    c = lax.axis_index("cd")
    i = lax.axis_index("ij")
    send = functools.partial(lax.ppermute, axis_name="cd")

    def tiles(shift, first, size):
        return lax.dynamic_slice(part, ((c + shift) % 4, first, 0, 0), (1, size, TILE, TILE))[0]

    rest = cap_z - half
    up_far = send(tiles(2, 0, half), perm=Z_UP)
    down_far = send(tiles(2, half, rest), perm=Z_DOWN)
    from_down = send(jnp.concatenate([tiles(1, 0, half) + up_far, tiles(1, half, rest)]), perm=Z_UP)
    from_up = send(jnp.concatenate([tiles(3, 0, half), tiles(3, half, rest) + down_far]), perm=Z_DOWN)
    total = tiles(0, 0, cap_z) + from_down + from_up
    high = jnp.minimum(first_rows[0], cap_z - cap_w)
    mine = lax.dynamic_slice_in_dim(total, jnp.where(i == 1, high, 0), cap_w)
    theirs = lax.dynamic_slice_in_dim(total, jnp.where(i == 1, 0, high), cap_w)
    other = lax.ppermute(theirs, "ij", [(0, 1), (1, 0)])
    return place(cap_z, cap_w, occ, outer, first_rows, mine, other)


def shards(amplitudes, integrals, occupied_label, outer_label, inner_label):
    others = lax.ppermute(amplitudes, "ab", CORE_SWAP)
    amp_pick, out_pick, first_rows = plan(occupied_label, outer_label, inner_label)
    packed = pack(occupied_label, inner_label, amplitudes, others)
    part = lax.switch(
        amp_pick[0],
        [functools.partial(gather_and_multiply, cap) for cap in CAPS_T],
        packed, occupied_label, outer_label, inner_label, integrals,
    )
    return lax.switch(
        out_pick[0],
        [functools.partial(reduce_and_place, caps) for caps in CAPS_R],
        part, occupied_label, outer_label, first_rows,
    )


def solution(mesh):
    placed = (P("ab", ("ij", "cd")), P("ab", ("ij", "cd")), P(), P(), P())
    return jax.shard_map(
        shards, mesh=mesh, in_specs=placed, out_specs=P(("ij", "cd"), "ab"), check_vma=False
    )
```

time: 689 us -> 175 us (0.25)
  blocking collectives: 379 us -> 0 us
  matrix products: 116 us -> 0 us
  waiting for transfers between devices: 150 us -> 100 us
  Pallas kernels: 0 us -> 46.7 us
  local copies, waits for them, and re-layouts: 19.6 us -> 3.19 us
  starting transfers between devices: 0.09 us -> 15.6 us
  between operations: 13.1 us -> 1.31 us
    all_to_all x1 -> x0, blocking collectives: 379 us -> none  [shards(): lax.all_to_all(all_rows, 'ij', split_axis=0, concat_axis=1, tiled=True)]
    dot_general x1 -> x0, matrix products: 116 us -> none  [contract(): lax.dot_general(left, right, (((1,), (1,)), ((), ())), precision=lax.Prec...]
    ppermute x0 -> x16, waiting for transfers between devices: none -> 100 us  [the longest x1 27.2 us: reduce_and_place(): send(jnp.concatenate([tiles(3, 0, half), tiles(3, half, rest) + down_far]...]
    all_gather x2 -> x0, waiting for transfers between devices: 99.1 us -> none  [the longest x1 99.1 us: shards(): all_rows = lax.all_gather(amp_masked, 'ab', axis=0, tiled=True)]
    reduce_scatter x1 -> x0, waiting for transfers between devices: 50.7 us -> none  [shards(): return lax.psum_scatter(partial_sum, 'cd', scatter_dimension=0, tiled=True)]
    pallas_call x0 -> x5, Pallas kernels: none -> 46.7 us  [the longest x1 32.6 us: ladder(): pl.pallas_call(functools.partial(ladder_kernel, cap), out_shape=jax.Shape...]
    all_to_all x1 -> x0, local copies, waits for them, and re-layouts: 18 us -> none  [shards(): lax.all_to_all(all_rows, 'ij', split_axis=0, concat_axis=1, tiled=True)]
    ppermute x0 -> x16, starting transfers between devices: none -> 15.6 us  [the longest x1 3.1 us: reduce_and_place(): send(jnp.concatenate([tiles(3, 0, half), tiles(3, half, rest) + down_far]...]
  transfers between devices with their start and end apart: 3 -> 16, of which waited for: 2 -> 11; matrix products, arithmetic and copies ran while one was open for 4% -> 0% of each run, Pallas kernels for 0% -> 6%
where the time goes in v1:
time: 175 us; the launch traced here: 173 us
  waiting for transfers between devices  100 us (57%)
  Pallas kernels  46.7 us (27%)
  starting transfers between devices  15.6 us (9%)
  other arithmetic  4.73 us (3%)
  local copies, waits for them, and re-layouts  3.19 us (2%)
    pallas_call x1, Pallas kernels, ladder(): pl.pallas_call(functools.partial(ladder_kernel, cap), out_shape=jax.Shape...  32.6 us
    ppermute x1, waiting for transfers between devices, reduce_and_place(): send(jnp.concatenate([tiles(3, 0, half), tiles(3, half, rest) + down_far]...  27.2 us
    ppermute x1, waiting for transfers between devices, reduce_and_place(): other = lax.ppermute(theirs, 'ij', [(0, 1), (1, 0)])  18.1 us
    ppermute x1, waiting for transfers between devices, reduce_and_place(): up_far = send(tiles(2, 0, half), perm=Z_UP)  14.2 us
    ppermute x1, waiting for transfers between devices, gather_and_multiply(): down_two = send(jnp.concatenate([x_own, down[half:]]), perm=Y_DOWN)  11.8 us
    ppermute x1, waiting for transfers between devices, gather_and_multiply(): down = send(own, perm=Y_DOWN)  11.6 us
    ppermute x1, waiting for transfers between devices, gather_and_multiply(): down_three = send(down_two[half:cap], perm=Y_DOWN)  6.88 us
    pallas_call x1, Pallas kernels, plan(): pl.pallas_call(plan_kernel, out_shape=(one, one, one), in_specs=[SMEM] *...  5.04 us
  transfers between devices with their start and end apart: 16, of which 11 were waited for; matrix products, arithmetic and copies ran while one was open for 0% of the time, Pallas kernels for 6%

profile of v1, /device:TPU:20, one launch (start us, length us, event | category | flops | bytes accessed | tf_op | source)
XLA Modules:
  0.0 173.1 jit_solution(15357476239051977276)
XLA Ops:
  0.0 5.0 %plan_capacities.1 = (s32[1]{0:T(128)}, s32[1]{0:T(128)}, s32[1]{0:T(128)}) custom-call(s32[16]{0:T(128)} %occ.3, s32[128]{0:T(128)} %outer.1, s32[128]{0:T(128)} %inner.3), custom_call_target="tpu_custom_call" | custom-call | tf_op jit(solution)/shard_map/plan_capacities/pallas_call | solution.py:90
  6.3 1.0 copy-done.2
  7.3 2.0 %pack_amplitudes.1 = f32[32,128,128]{2,1,0:T(8,128)S(1)} custom-call(s32[16]{0:T(128)} %occ.3, s32[128]{0:T(128)} %inner.3, f32[128,2048]{1,0:T(8,128)} %mine.1, f32[128,2048]{1,0:T(8,128)} %copy-done.2), custom_call_target="tpu_custom_call" | custom-call | tf_op jit(solution)/shard_map/pack_amplitudes/pallas_call | solution.py:135
  9.4 84.5 %conditional.2 = (f32[4,32,128,128]{3,2,1,0:T(8,128)}) conditional(s32[]{:T(128)} %bitcast.33, (f32[32,128,128]{2,1,0:T(8,128)S(1)}, s32[128]{0:T(128)S(1)}, s32[128]{0:T(128)S(1)}, f32[1024,2048]{1,0:T(8,128)}, s32[16]{0:T(128)S(1)}) %tuple.79, (f32[32,128,128]{2,1,0:T(8,128)S(1)}, s32[128]{0:T(128)S(1)}, s32[128]{0:T(128)S(1)}, ...), branch_computations={%region_0.1_spmd, %region_1.2_spmd, %region_2.3_spmd} | conditional | flops 20185088 | bytes 152044160 | solution.py:485
  9.4 0.5 collective-permute-start.3
  10.0 1.6 collective-permute-start.1
  11.5 0.7 collective-permute-start
  12.2 11.6 %collective-permute-done.3.refs_3_ = f32[8,128,128]{2,1,0:T(8,128)S(1)} collective-permute-done((f32[8,128,128]{2,1,0:T(8,128)S(1)}, f32[8,128,128]{2,1,0:T(8,128)S(1)}, u32[]{:S(2)}, u32[]{:S(2)}) %collective-permute-start.3) | collective-permute-done | bytes 524320 | tf_op jit(solution)/shard_map/cond/branch_0_fun/ppermute | solution.py:417
  24.0 2.8 %collective-permute-done.refs_1_ = f32[8,128,128]{2,1,0:T(8,128)S(1)} collective-permute-done((f32[8,128,128]{2,1,0:T(8,128)S(1)}, f32[8,128,128]{2,1,0:T(8,128)S(1)}, u32[]{:S(2)}, u32[]{:S(2)}) %collective-permute-start) | collective-permute-done | bytes 524320 | tf_op jit(solution)/shard_map/cond/branch_0_fun/ppermute | solution.py:415
  26.8 0.2 pad_maximum_fusion.2
  27.0 0.5 collective-permute-start.4
  27.5 2.4 %collective-permute-start.2 = (f32[12,128,128]{2,1,0:T(8,128)S(1)}, f32[12,128,128]{2,1,0:T(8,128)S(1)}, u32[]{:S(2)}, u32[]{:S(2)}) collective-permute-start(f32[12,128,128]{2,1,0:T(8,128)S(1)} %get-tuple-element.133), channel_id=1, source_target_pairs={{0,16},{4,20},{8,24},{12,28},{16,32},{20,36},{24,40},{28,44},{32,4... | collective-permute-start | bytes 2359304 | tf_op jit(solution)/shard_map/cond/branch_0_fun/ppermute | solution.py:418
  29.9 4.7 %split_integrals.3 = (bf16[128,128,128]{2,1,0:T(8,128)(2,1)S(1)}, bf16[128,128,128]{2,1,0:T(8,128)(2,1)S(1)}) custom-call(s32[128]{0:T(128)S(1)} %get-tuple-element.70.outer, s32[128]{0:T(128)S(1)} %get-tuple-element.76.inner, f32[1024,2048]{1,0:T(8,128)} %get-tuple-element.80.ints), custom_call_target="tpu_custom_call" | custom-call | flops 16777216 | bytes 16777216 | tf_op jit(solution)/shard_map/cond/branch_0_fun/split_integrals/pallas_call | solution.py:198
  34.9 11.8 %collective-permute-done.4.refs_5_ = f32[12,128,128]{2,1,0:T(8,128)S(1)} collective-permute-done((f32[12,128,128]{2,1,0:T(8,128)S(1)}, f32[12,128,128]{2,1,0:T(8,128)S(1)}, u32[]{:S(2)}, u32[]{:S(2)}) %collective-permute-start.4) | collective-permute-done | bytes 786464 | tf_op jit(solution)/shard_map/cond/branch_0_fun/ppermute | solution.py:419
  46.9 2.4 %collective-permute-start.6 = (f32[4,128,128]{2,1,0:T(8,128)S(1)}, f32[4,128,128]{2,1,0:T(8,128)S(1)}, u32[]{:S(2)}, u32[]{:S(2)}) collective-permute-start(f32[4,128,128]{2,1,0:T(8,128)S(1)} %slice.27), channel_id=1, source_target_pairs={{0,48},{4,52},{8,56},{12,60},{16,0},{20,4},{24,8},{28,12},{32,16},... | collective-permute-start | bytes 786440 | tf_op jit(solution)/shard_map/cond/branch_0_fun/ppermute | solution.py:423
  49.4 0.7 collective-permute-start.5
  50.0 6.9 %collective-permute-done.6.refs_7_ = f32[4,128,128]{2,1,0:T(8,128)S(1)} collective-permute-done((f32[4,128,128]{2,1,0:T(8,128)S(1)}, f32[4,128,128]{2,1,0:T(8,128)S(1)}, u32[]{:S(2)}, u32[]{:S(2)}) %collective-permute-start.6) | collective-permute-done | bytes 262176 | tf_op jit(solution)/shard_map/cond/branch_0_fun/ppermute | solution.py:423
  56.9 2.1 %collective-permute-done.5.refs_6_ = f32[4,128,128]{2,1,0:T(8,128)S(1)} collective-permute-done((f32[4,128,128]{2,1,0:T(8,128)S(1)}, f32[4,128,128]{2,1,0:T(8,128)S(1)}, u32[]{:S(2)}, u32[]{:S(2)}) %collective-permute-start.5) | collective-permute-done | bytes 262176 | tf_op jit(solution)/shard_map/cond/branch_0_fun/ppermute | solution.py:422
  59.1 1.9 %collective-permute-done.9.refs_10_ = f32[8,128,128]{2,1,0:T(8,128)S(1)} collective-permute-done((f32[8,128,128]{2,1,0:T(8,128)S(1)}, f32[8,128,128]{2,1,0:T(8,128)S(1)}, u32[]{:S(2)}, u32[]{:S(2)}) %collective-permute-start.9) | collective-permute-done | bytes 524320 | tf_op jit(solution)/shard_map/cond/branch_0_fun/ppermute | solution.py:427
  61.0 32.6 %ladder_tiles.3 = f32[4,32,128,128]{3,2,1,0:T(8,128)} custom-call(s32[16]{0:T(128)S(1)} %get-tuple-element.69.occ, s32[128]{0:T(128)S(1)} %get-tuple-element.70.outer, s32[128]{0:T(128)S(1)} %get-tuple-element.76.inner, bf16[128,128,128]{2,1,0:T(8,128)(2,1)S(1)} %get-tuple-element.83.ints_hi, bf16[128,128,128]{2,1,0:T(8,128)(2,1)S(1)} %get-tuple-element.84.ints_lo, ...), custom_call_target="tpu_custom_call" | custom-call | tf_op jit(solution)/shard_map/cond/branch_0_fun/ladder_tiles/pallas_call | solution.py:386
  93.9 79.2 %conditional.3 = (f32[256,1024]{1,0:T(8,128)}) conditional(s32[]{:T(128)} %bitcast.32, (f32[4,32,128,128]{3,2,1,0:T(8,128)}, s32[1]{0:T(128)}, s32[16]{0:T(128)S(1)}, s32[128]{0:T(128)S(1)}) %tuple.75, (f32[4,32,128,128]{3,2,1,0:T(8,128)}, s32[1]{0:T(128)}, s32[16]{0:T(128)S(1)}, s32[128]{0:T(128)S(1)}) %tuple.76, ...), branch_computations={%region_3.4_spmd, %region_4.5_spmd, %region_5.6_spmd, %region_6.7_... | conditional | flops 2621514 | bytes 65012712 | solution.py:490
  94.0 2.0 %dynamic-slice_bitcast_fusion.11 = (f32[11,128,128]{2,1,0:T(8,128)S(1)}, f32[11,128,128]{2,1,0:T(8,128)S(1)}, f32[11,128,128]{2,1,0:T(8,128)S(1)}, f32[11,128,128]{2,1,0:T(8,128)S(1)}) fusion(f32[4,32,128,128]{3,2,1,0:T(8,128)} %get-tuple-element.120, s32[]{:T(128)S(6)} %select_n.203, s32[]{:T(128)S(6)} %select_n.205, s32[]{:T(128)S(6)} %select_n.201), kind=kLoop, calls=%fused_computation.51 | loop fusion | bytes 5767180 | tf_op jit(solution)/shard_map/cond/branch_2_fun/squeeze | solution.py:466
  95.9 1.0 collective-permute-start.40
  96.9 2.3 %collective-permute-start.42 = (f32[11,128,128]{2,1,0:T(8,128)S(1)}, f32[11,128,128]{2,1,0:T(8,128)S(1)}, u32[]{:S(2)}, u32[]{:S(2)}) collective-permute-start(f32[11,128,128]{2,1,0:T(8,128)S(1)} %get-tuple-element.157), channel_id=1, source_target_pairs={{0,3},{1,0},{2,1},{3,2},{4,7},{5,4},{6,5},{7,6},{8,11},{9,8},{10,9... | collective-permute-start | bytes 2162696 | tf_op jit(solution)/shard_map/cond/branch_2_fun/ppermute | solution.py:470
  99.2 14.2 %collective-permute-done.40 = f32[11,128,128]{2,1,0:T(8,128)S(1)} collective-permute-done((f32[11,128,128]{2,1,0:T(8,128)S(1)}, f32[11,128,128]{2,1,0:T(8,128)S(1)}, u32[]{:S(2)}, u32[]{:S(2)}) %collective-permute-start.40) | collective-permute-done | bytes 720928 | tf_op jit(solution)/shard_map/cond/branch_2_fun/ppermute | solution.py:469
  113.4 1.5 bitcast_add_fusion.8
  115.1 3.1 %collective-permute-start.43 = (f32[22,128,128]{2,1,0:T(8,128)S(1)}, f32[22,128,128]{2,1,0:T(8,128)}, u32[]{:S(2)}, u32[]{:S(2)}) collective-permute-start(f32[22,128,128]{2,1,0:T(8,128)S(1)} %pad_maximum_fusion.20), channel_id=1, source_target_pairs={{0,3},{1,0},{2,1},{3,2},{4,7},{5,4},{6,5},{7,6},{8,11},{9,8},{10,9... | collective-permute-start | bytes 4325384 | tf_op jit(solution)/shard_map/cond/branch_2_fun/ppermute | solution.py:472
  119.1 27.2 %collective-permute-done.43 = f32[22,128,128]{2,1,0:T(8,128)} collective-permute-done((f32[22,128,128]{2,1,0:T(8,128)S(1)}, f32[22,128,128]{2,1,0:T(8,128)}, u32[]{:S(2)}, u32[]{:S(2)}) %collective-permute-start.43) | collective-permute-done | bytes 1441824 | tf_op jit(solution)/shard_map/cond/branch_2_fun/ppermute | solution.py:472
  146.3 3.7 %collective-permute-done.41 = f32[22,128,128]{2,1,0:T(8,128)} collective-permute-done((f32[22,128,128]{2,1,0:T(8,128)S(1)}, f32[22,128,128]{2,1,0:T(8,128)}, u32[]{:S(2)}, u32[]{:S(2)}) %collective-permute-start.41) | collective-permute-done | bytes 1441824 | tf_op jit(solution)/shard_map/cond/branch_2_fun/ppermute | solution.py:471
  150.0 2.5 %fusion.2 = f32[22,128,128]{2,1,0:T(8,128)S(1)} fusion(f32[22,128,128]{2,1,0:T(8,128)} %collective-permute-done.43, f32[22,128,128]{2,1,0:T(8,128)} %collective-permute-done.41, f32[4,32,128,128]{3,2,1,0:T(8,128)} %get-tuple-element.120, s32[]{:T(128)S(6)} %select_n.199), kind=kLoop, calls=%fused_computation.45 | loop fusion | flops 720896 | bytes 5767172 | tf_op jit(solution)/shard_map/cond/branch_2_fun/add | solution.py:473
  152.7 18.1 %collective-permute-done.44.other = f32[14,128,128]{2,1,0:T(8,128)S(1)} collective-permute-done((f32[14,128,128]{2,1,0:T(8,128)S(1)}, f32[14,128,128]{2,1,0:T(8,128)S(1)}, u32[]{:S(2)}, u32[]{:S(2)}) %collective-permute-start.44) | collective-permute-done | bytes 917536 | tf_op jit(solution)/shard_map/cond/branch_2_fun/ppermute | solution.py:477
  170.8 2.3 %place_tiles.6 = f32[256,1024]{1,0:T(8,128)} custom-call(s32[16]{0:T(128)S(1)} %get-tuple-element.117.occ, s32[128]{0:T(128)S(1)} %get-tuple-element.118.outer, s32[1]{0:T(128)} %get-tuple-element.119.first_rows, f32[14,128,128]{2,1,0:T(8,128)S(1)} %get-tuple-element.161.mine, f32[14,128,128]{2,1,0:T(8,128)S(1)} %collective-permute-done.44.other), custom_call_target="tpu_custom_call" | custom-call | tf_op jit(solution)/shard_map/cond/branch_2_fun/place_tiles/pallas_call | solution.py:448
  (30 shorter events, 1.4 us)
Async XLA Ops:
  0.0 6.3 %collective-permute-start.50 = (f32[128,2048]{1,0:T(8,128)}, f32[128,2048]{1,0:T(8,128)S(1)}, u32[]{:S(2)}, u32[]{:S(2)}) collective-permute-start(f32[128,2048]{1,0:T(8,128)} %mine.1), channel_id=1, source_target_pairs={{0,4},{4,0},{8,12},{12,8},{16,20},{20,16},{24,28},{28,24},{32,36},... | collective-permute-start | bytes 3145736 | tf_op jit(solution)/shard_map/ppermute | solution.py:482
  6.3 3.1 %copy-start.3 = (s32[128]{0:T(128)S(1)}, s32[128]{0:T(128)}, u32[]{:S(2)}) copy-start(s32[128]{0:T(128)} %outer.1) | copy-start | bytes 1540
  6.3 3.1 %copy-start.4 = (s32[16]{0:T(128)S(1)}, s32[16]{0:T(128)}, u32[]{:S(2)}) copy-start(s32[16]{0:T(128)} %occ.3) | copy-start | bytes 196
  6.3 3.1 %copy-start.5 = (s32[128]{0:T(128)S(1)}, s32[128]{0:T(128)}, u32[]{:S(2)}) copy-start(s32[128]{0:T(128)} %inner.3) | copy-start | bytes 1540
  6.3 1.0 copy-start.2
  9.4 14.4 %collective-permute-start.3 = (f32[8,128,128]{2,1,0:T(8,128)S(1)}, f32[8,128,128]{2,1,0:T(8,128)S(1)}, u32[]{:S(2)}, u32[]{:S(2)}) collective-permute-start(f32[8,128,128]{2,1,0:T(8,128)S(1)} %constant_dynamic-slice_fusion), channel_id=1, source_target_pairs={{0,48},{4,52},{8,56},{12,60},{16,0},{20,4},{24,8},{28,12},{32,16},... | collective-permute-start | bytes 1572872 | tf_op jit(solution)/shard_map/cond/branch_0_fun/ppermute | solution.py:417
  10.0 14.1 %collective-permute-start.1 = (f32[8,128,128]{2,1,0:T(8,128)S(1)}, f32[8,128,128]{2,1,0:T(8,128)S(1)}, u32[]{:S(2)}, u32[]{:S(2)}) collective-permute-start(f32[8,128,128]{2,1,0:T(8,128)S(1)} %constant_dynamic-slice_fusion), channel_id=1, source_target_pairs={{0,16},{4,20},{8,24},{12,28},{16,32},{20,36},{24,40},{28,44},{32,4... | collective-permute-start | bytes 1572872 | tf_op jit(solution)/shard_map/cond/branch_0_fun/ppermute | solution.py:416
  11.5 15.3 %collective-permute-start = (f32[8,128,128]{2,1,0:T(8,128)S(1)}, f32[8,128,128]{2,1,0:T(8,128)S(1)}, u32[]{:S(2)}, u32[]{:S(2)}) collective-permute-start(f32[8,128,128]{2,1,0:T(8,128)S(1)} %constant_dynamic-slice_fusion), channel_id=1, source_target_pairs={{0,8},{4,12},{8,0},{12,4},{16,24},{20,28},{24,16},{28,20},{32,40},... | collective-permute-start | bytes 1572872 | tf_op jit(solution)/shard_map/cond/branch_0_fun/ppermute | solution.py:415
  27.0 19.6 %collective-permute-start.4 = (f32[12,128,128]{2,1,0:T(8,128)S(1)}, f32[12,128,128]{2,1,0:T(8,128)S(1)}, u32[]{:S(2)}, u32[]{:S(2)}) collective-permute-start(f32[12,128,128]{2,1,0:T(8,128)S(1)} %get-tuple-element.132), channel_id=1, source_target_pairs={{0,48},{4,52},{8,56},{12,60},{16,0},{20,4},{24,8},{28,12},{32,16},... | collective-permute-start | bytes 2359304 | tf_op jit(solution)/shard_map/cond/branch_0_fun/ppermute | solution.py:419
  27.5 19.1 %collective-permute-start.2 = (f32[12,128,128]{2,1,0:T(8,128)S(1)}, f32[12,128,128]{2,1,0:T(8,128)S(1)}, u32[]{:S(2)}, u32[]{:S(2)}) collective-permute-start(f32[12,128,128]{2,1,0:T(8,128)S(1)} %get-tuple-element.133), channel_id=1, source_target_pairs={{0,16},{4,20},{8,24},{12,28},{16,32},{20,36},{24,40},{28,44},{32,4... | collective-permute-start | bytes 2359304 | tf_op jit(solution)/shard_map/cond/branch_0_fun/ppermute | solution.py:418
  34.8 24.3 %collective-permute-start.7 = (f32[24,128,128]{2,1,0:T(8,128)S(1)}, f32[24,128,128]{2,1,0:T(8,128)S(1)}, u32[]{:S(2)}, u32[]{:S(2)}) collective-permute-start(f32[24,128,128]{2,1,0:T(8,128)S(1)} %pad_maximum_fusion), channel_id=1, source_target_pairs={{0,4},{4,0},{8,12},{12,8},{16,20},{20,16},{24,28},{28,24},{32,36},... | collective-permute-start | bytes 4718600 | tf_op jit(solution)/shard_map/cond/branch_0_fun/ppermute | solution.py:425
  46.8 14.2 %collective-permute-start.8 = (f32[24,128,128]{2,1,0:T(8,128)S(1)}, f32[24,128,128]{2,1,0:T(8,128)S(1)}, u32[]{:S(2)}, u32[]{:S(2)}) collective-permute-start(f32[24,128,128]{2,1,0:T(8,128)S(1)} %pad_maximum_fusion.1), channel_id=1, source_target_pairs={{0,4},{4,0},{8,12},{12,8},{16,20},{20,16},{24,28},{28,24},{32,36},... | collective-permute-start | bytes 4718600 | tf_op jit(solution)/shard_map/cond/branch_0_fun/ppermute | solution.py:426
  46.9 10.0 %collective-permute-start.6 = (f32[4,128,128]{2,1,0:T(8,128)S(1)}, f32[4,128,128]{2,1,0:T(8,128)S(1)}, u32[]{:S(2)}, u32[]{:S(2)}) collective-permute-start(f32[4,128,128]{2,1,0:T(8,128)S(1)} %slice.27), channel_id=1, source_target_pairs={{0,48},{4,52},{8,56},{12,60},{16,0},{20,4},{24,8},{28,12},{32,16},... | collective-permute-start | bytes 786440 | tf_op jit(solution)/shard_map/cond/branch_0_fun/ppermute | solution.py:423
  49.4 9.6 %collective-permute-start.5 = (f32[4,128,128]{2,1,0:T(8,128)S(1)}, f32[4,128,128]{2,1,0:T(8,128)S(1)}, u32[]{:S(2)}, u32[]{:S(2)}) collective-permute-start(f32[4,128,128]{2,1,0:T(8,128)S(1)} %slice.26), channel_id=1, source_target_pairs={{0,16},{4,20},{8,24},{12,28},{16,32},{20,36},{24,40},{28,44},{32,4... | collective-permute-start | bytes 786440 | tf_op jit(solution)/shard_map/cond/branch_0_fun/ppermute | solution.py:422
  59.0 2.0 %collective-permute-start.9 = (f32[8,128,128]{2,1,0:T(8,128)S(1)}, f32[8,128,128]{2,1,0:T(8,128)S(1)}, u32[]{:S(2)}, u32[]{:S(2)}) collective-permute-start(f32[8,128,128]{2,1,0:T(8,128)S(1)} %pad_maximum_fusion.4), channel_id=1, source_target_pairs={{0,4},{4,0},{8,12},{12,8},{16,20},{20,16},{24,28},{28,24},{32,36},... | collective-permute-start | bytes 1572872 | tf_op jit(solution)/shard_map/cond/branch_0_fun/ppermute | solution.py:427
  95.9 17.5 %collective-permute-start.40 = (f32[11,128,128]{2,1,0:T(8,128)S(1)}, f32[11,128,128]{2,1,0:T(8,128)S(1)}, u32[]{:S(2)}, u32[]{:S(2)}) collective-permute-start(f32[11,128,128]{2,1,0:T(8,128)S(1)} %get-tuple-element.156), channel_id=1, source_target_pairs={{0,1},{1,2},{2,3},{3,0},{4,5},{5,6},{6,7},{7,4},{8,9},{9,10},{10,1... | collective-permute-start | bytes 2162696 | tf_op jit(solution)/shard_map/cond/branch_2_fun/ppermute | solution.py:469
  96.9 16.5 %collective-permute-start.42 = (f32[11,128,128]{2,1,0:T(8,128)S(1)}, f32[11,128,128]{2,1,0:T(8,128)S(1)}, u32[]{:S(2)}, u32[]{:S(2)}) collective-permute-start(f32[11,128,128]{2,1,0:T(8,128)S(1)} %get-tuple-element.157), channel_id=1, source_target_pairs={{0,3},{1,0},{2,1},{3,2},{4,7},{5,4},{6,5},{7,6},{8,11},{9,8},{10,9... | collective-permute-start | bytes 2162696 | tf_op jit(solution)/shard_map/cond/branch_2_fun/ppermute | solution.py:470
  115.1 31.2 %collective-permute-start.43 = (f32[22,128,128]{2,1,0:T(8,128)S(1)}, f32[22,128,128]{2,1,0:T(8,128)}, u32[]{:S(2)}, u32[]{:S(2)}) collective-permute-start(f32[22,128,128]{2,1,0:T(8,128)S(1)} %pad_maximum_fusion.20), channel_id=1, source_target_pairs={{0,3},{1,0},{2,1},{3,2},{4,7},{5,4},{6,5},{7,6},{8,11},{9,8},{10,9... | collective-permute-start | bytes 4325384 | tf_op jit(solution)/shard_map/cond/branch_2_fun/ppermute | solution.py:472
  118.3 31.6 %collective-permute-start.41 = (f32[22,128,128]{2,1,0:T(8,128)S(1)}, f32[22,128,128]{2,1,0:T(8,128)}, u32[]{:S(2)}, u32[]{:S(2)}) collective-permute-start(f32[22,128,128]{2,1,0:T(8,128)S(1)} %pad_maximum_fusion.19), channel_id=1, source_target_pairs={{0,1},{1,2},{2,3},{3,0},{4,5},{5,6},{6,7},{7,4},{8,9},{9,10},{10,1... | collective-permute-start | bytes 4325384 | tf_op jit(solution)/shard_map/cond/branch_2_fun/ppermute | solution.py:471
  152.6 18.2 %collective-permute-start.44 = (f32[14,128,128]{2,1,0:T(8,128)S(1)}, f32[14,128,128]{2,1,0:T(8,128)S(1)}, u32[]{:S(2)}, u32[]{:S(2)}) collective-permute-start(f32[14,128,128]{2,1,0:T(8,128)S(1)} %get-tuple-element.160), channel_id=1, source_target_pairs={{0,64},{64,0},{1,65},{65,1},{2,66},{66,2},{3,67},{67,3},{4,68},{68... | collective-permute-start | bytes 2752520 | tf_op jit(solution)/shard_map/cond/branch_2_fun/ppermute | solution.py:477
